TPU v7x, 32 devices: a whole 2x2x4 slice. The times are simulated.
32 devices in a mesh: row: 8 (over y, x, core), orb: 4 (over z).
Axes of the slice: x: 2, y: 2, z: 4, core: 2. Of those that a mesh axis runs over, the one named last changes fastest.
Arguments:
- chol_vectors: bfloat16 [4, 8192, 8192], P(None, 'row', 'orb'), may hold values from -6 to 6
- orbitals: bfloat16 [8192, 1024], P('orb'), may hold values from -0.0078125 to 0.0078125
Outputs:
- exchange: float32 [8192, 8192], P(('row', 'orb'))
All inputs are finite; a program needn't handle non-finite values.
Results may differ from a plain program's by a relative error of at most 0.0032.
Values may be sent and summed in bfloat16 or wider, within the bound.
A program may use at most 128 MiB of HBM per device.

v0:
```python
import jax
import jax.numpy as jnp
from jax import lax
from jax.sharding import PartitionSpec as P


def tile_product(left, right):
    return lax.dot_general(
        left, right, (((0,), (0,)), ((), ())), preferred_element_type=jnp.float32
    )


def on_device(chol_vectors, orbitals):
    vectors, row_count, contracted = chol_vectors.shape
    orbital_count = orbitals.shape[1]
    orb_count = lax.axis_size("orb")
    own_orbitals = orbital_count // orb_count
    term = jnp.einsum("mi,prm->ipr", orbitals, chol_vectors, preferred_element_type=jnp.float32)
    summed = lax.psum_scatter(
        term.reshape(own_orbitals * lax.axis_size("orb"), vectors * row_count),
        "orb",
        scatter_dimension=0,
        tiled=True,
    )
    blocks_local = summed.astype(jnp.bfloat16).reshape(own_orbitals * vectors, row_count)
    partial_value = tile_product(
        blocks_local, lax.all_gather(blocks_local, "row", axis=1, tiled=True)
    )
    return lax.psum_scatter(partial_value, "orb", scatter_dimension=0, tiled=True)


def solution(mesh):
    return jax.shard_map(
        on_device,
        mesh=mesh,
        in_specs=(P(None, "row", "orb"), P("orb", None)),
        out_specs=P(("row", "orb"), None),
        check_vma=False,
    )
```

profile of v0, /device:TPU:0, one launch (start us, length us, event | category | flops | bytes accessed | tf_op | source)
XLA Modules:
  0.0 1012.8 jit_solution(2220032901056871014)
XLA Ops:
  6.5 0.0 reduce-scatter.3.cloned.1.call-start
  6.5 23.5 %fusion = f32[1024,4,1024]{0,2,1:T(8,128)} fusion(bf16[4,1024,2048]{2,1,0:T(8,128)(2,1)} %param.2, bf16[2048,1024]{1,0:T(8,128)(2,1)} %param.3), kind=kOutput, calls=%fused_computation | convolution fusion | flops 17179869184 | bytes 37748736 | tf_op jit(solution)/shard_map/mi,prm->ipr/dot_general | solution.py:18
  30.0 17.5 %copy.3 = f32[1024,4096]{1,0:T(8,128)} copy(f32[1024,4096]{0,1:T(8,128)} %bitcast.7) | data formatting | bytes 33554432 | tf_op jit(solution)/shard_map/reshape | solution.py:20
  47.5 0.0 reduce-scatter.3.cloned.1.call-update
  47.5 0.0 all-gather.2.cloned.1.call-start
  47.6 283.1 %reduce-scatter.3.cloned.1.call-done = f32[256,4096]{1,0:T(8,128)} async-done(((f32[1024,4096]{1,0:T(8,128)}), f32[256,4096]{1,0:T(8,128)}) %reduce-scatter.3.cloned.1.call-update) | async-done | bytes 4194320 | tf_op jit(solution)/shard_map/reduce_scatter | solution.py:19
  330.7 2.5 convert_element_type.3
  333.1 2.6 reshape.7
  335.7 0.0 all-gather.2.cloned.1.call-update
  335.7 0.2 reduce-scatter.5.cloned.1.call-start
  335.9 90.5 %all-gather.2.cloned.1.call-done = bf16[1024,8192]{1,0:T(8,128)(2,1)} async-done(((bf16[1024,1024]{1,0:T(8,128)(2,1)}), bf16[1024,8192]{1,0:T(8,128)(2,1)}) %all-gather.2.cloned.1.call-update) | async-done | bytes 16777232 | tf_op jit(solution)/shard_map/all_gather | solution.py:27
  426.5 27.6 %fusion.2 = f32[1024,8192]{1,0:T(8,128)} fusion(bf16[1024,1024]{1,0:T(8,128)(2,1)} %reshape.7, bf16[1024,8192]{1,0:T(8,128)(2,1)} %all-gather.2.cloned.1.call-done), kind=kOutput, calls=%fused_computation.2 | convolution fusion | flops 17179869184 | bytes 52428800 | tf_op jit(solution)/shard_map/dot_general | solution.py:8
  454.1 0.0 reduce-scatter.5.cloned.1.call-update
  454.1 552.2 %reduce-scatter.5.cloned.1.call-done = f32[256,8192]{1,0:T(8,128)} async-done(((f32[1024,8192]{1,0:T(8,128)}), f32[256,8192]{1,0:T(8,128)}) %reduce-scatter.5.cloned.1.call-update) | async-done | bytes 8388624 | tf_op jit(solution)/shard_map/reduce_scatter | solution.py:29
Async XLA Ops:
  6.5 324.1 %reduce-scatter.3.cloned.1.call-start = ((), (), s32[]{:S(2)}) async-start(), calls=%async_computation.2 | async-start | bytes 20971520 | tf_op jit(solution)/shard_map/reduce_scatter | solution.py:19
  47.5 379.0 %all-gather.2.cloned.1.call-start = ((), (), s32[]{:S(2)}) async-start(), calls=%async_computation.3 | async-start | bytes 18874368 | tf_op jit(solution)/shard_map/all_gather | solution.py:27
  335.7 670.6 %reduce-scatter.5.cloned.1.call-start = ((), (), s32[]{:S(2)}) async-start(), calls=%async_computation.4 | async-start | bytes 41943040 | tf_op jit(solution)/shard_map/reduce_scatter | solution.py:29
Sparse Core Ops, SparseCore 0:
  47.6 282.9 reduce-scatter.2
  335.8 90.5 all-gather.1
  454.2 552.0 reduce-scatter.4
where the time goes:
time: 1010 us
  waiting for transfers between devices  926 us (92%)
  matrix products  51.1 us (5%)
  local copies, waits for them, and re-layouts  20 us (2%)
  between operations  13.1 us (1%)
    reduce_scatter x1, waiting for transfers between devices, on_device(): lax.psum_scatter(partial_value, 'orb', scatter_dimension=0, tiled=True)  552 us
    reduce_scatter x1, waiting for transfers between devices, on_device(): lax.psum_scatter(term.reshape(own_orbitals * lax.axis_size('orb'), vector...  283 us
    all_gather x1, waiting for transfers between devices, on_device(): lax.all_gather(blocks_local, 'row', axis=1, tiled=True)  90.5 us
    dot_general x1, matrix products, tile_product(): lax.dot_general(left, right, (((0,), (0,)), ((), ())), preferred_element_...  27.6 us
    dot_general x1, matrix products, on_device(): jnp.einsum('mi,prm->ipr', orbitals, chol_vectors, preferred_element_type=...  23.5 us
  transfers between devices with their start and end apart: 3, of which 3 were waited for; matrix products, arithmetic and copies ran while one was open for 0% of the time, Pallas kernels for 0%

commit v1 on v0

v1 whole, which is shorter than its diff:
```python
import functools

import jax
import jax.numpy as jnp
from jax import lax
from jax.experimental import pallas as pl
from jax.experimental.pallas import tpu as pltpu
from jax.sharding import PartitionSpec as P

MESH = pl.DeviceIdType.MESH
CORES = 2
SPLIT = 2


def snake(place, count):
    half = count // 2
    return place + (place // half) * (half + count - 1 - 2 * place)


def gather_kernel(
    sizes, terms, own, out, stage, landed,
    sum_s, sum_r, up_s, down_s, line_r, ring_s, ring_r, pair_s, pair_r, local_s,
):
    row_n, orb_n, split = sizes
    chips = row_n // CORES
    vectors, block, count = own.shape
    width = count // split
    chunks = vectors * split
    row, z = lax.axis_index("row"), lax.axis_index("orb")
    core = row % CORES
    place = snake(row // CORES, chips)

    def at(step):
        return snake((place + step + chips) % chips, chips) * CORES + core

    onward, back = at(1), at(-1)
    other = row + 1 - 2 * core

    barrier = pltpu.get_barrier_semaphore()
    peers = [(row, (z + d) % orb_n) for d in range(1, orb_n)]
    peers += [(onward, z), (back, z), (other, z)]
    for peer in peers:
        pl.semaphore_signal(barrier, inc=1, device_id=peer, device_id_type=MESH)
    pl.semaphore_wait(barrier, len(peers))

    def columns(k):
        return pl.ds(pl.multiple_of(k * width, width), width)

    def part(k, r, q):
        return out.at[pl.ds(pl.multiple_of((r * orb_n + q) * block, block), block), columns(k)]

    def column(k, r):
        rows = orb_n * block
        return out.at[pl.ds(pl.multiple_of(r * rows, rows), rows), columns(k)]

    def remote(src, dst, send, recv, device):
        return pltpu.make_async_remote_copy(
            src_ref=src, dst_ref=dst, send_sem=send, recv_sem=recv, device_id=device, device_id_type=MESH
        )

    def scatter(k, d):
        to = (z + d) % orb_n
        src = terms.at[k // split, pl.ds(pl.multiple_of(to * block, block), block), columns(k % split)]
        return remote(src, landed.at[k, d - 1], sum_s.at[k, d - 1], sum_r.at[k, d - 1], (row, to))

    def line(k, q, up, first=False):
        src = stage.at[k] if first else part(k, row, q)
        send = up_s.at[k, q] if up else down_s.at[k, q]
        return remote(src, part(k, row, q), send, line_r.at[k, q], (row, z + 1 if up else z - 1))

    def keep(k):
        return pltpu.make_async_copy(stage.at[k], part(k, row, z), local_s.at[k])

    def ring(k, hop, side):
        r = at(-(hop - 1)) if side == 0 else at(hop - 1)
        j = hop if side == 0 else chips - hop
        return remote(
            column(k, r), column(k, r), ring_s.at[k, side, hop - 1], ring_r.at[k, j],
            (onward if side == 0 else back, z),
        )

    def arrived(k, hop, side):
        r = at(-hop) if side == 0 else at(hop)
        j = hop if side == 0 else chips - hop
        remote(
            column(k, r), column(k, r), ring_s.at[k, side, hop - 1], ring_r.at[k, j],
            (onward if side == 0 else back, z),
        ).wait_recv()
        pair(k, j).start()

    def pair(k, j):
        r = at(-j)
        return remote(column(k, r), column(k, r), pair_s.at[k, j], pair_r.at[k, j], (other, z))

    def pair_in(k, j):
        r = at(-j) + 1 - 2 * core
        return remote(column(k, r), column(k, r), pair_s.at[k, j], pair_r.at[k, j], (other, z))

    hops = chips // 2

    def on_side(k, hop, side, act):
        if hop < hops:
            act()
        else:
            pl.when(k % 2 == side)(act)

    def total(k):
        rows = 32
        def one(i, carry):
            at_rows = pl.ds(pl.multiple_of(i * rows, rows), rows)
            value = own[k // split, at_rows, columns(k % split)]
            for d in range(orb_n - 1):
                value = value + landed[k, d, at_rows, :].astype(jnp.float32)
            stage[k, at_rows, :] = value.astype(jnp.bfloat16)
            return carry
        lax.fori_loop(0, block // rows, one, 0)

    for d in range(1, orb_n):
        scatter(0, d).start()

    def step(t, carry):
        before = t - 1

        @pl.when(t < chunks - 1)
        def _():
            for d in range(1, orb_n):
                scatter(t + 1, d).start()

        @pl.when(t < chunks)
        def _():
            for d in range(1, orb_n):
                scatter(t, d).wait_recv()
            total(t)
            keep(t).start()
            pl.when(z + 1 < orb_n)(lambda: line(t, z, True, True).start())
            pl.when(z >= 1)(lambda: line(t, z, False, True).start())

        @pl.when(t >= 1)
        def _():
            for hop in range(1, hops):
                for side in (0, 1):
                    arrived(before, hop, side)
                    on_side(before, hop + 1, side, lambda: ring(before, hop + 1, side).start())

        @pl.when(t < chunks)
        def _():
            for h in range(1, orb_n):
                @pl.when(z - h >= 0)
                def _():
                    line(t, z - h, True).wait_recv()
                    pl.when(z + 1 < orb_n)(lambda: line(t, z - h, True).start())

                @pl.when(z + h < orb_n)
                def _():
                    line(t, z + h, False).wait_recv()
                    pl.when(z >= 1)(lambda: line(t, z + h, False).start())
            keep(t).wait()
            for side in (0, 1):
                on_side(t, 1, side, lambda: ring(t, 1, side).start())
            pair(t, 0).start()

        @pl.when(t >= 1)
        def _():
            for side in (0, 1):
                on_side(before, hops, side, lambda: arrived(before, hops, side))

        return carry

    lax.fori_loop(0, chunks + 1, step, 0)

    def finish(k, carry):
        for d in range(1, orb_n):
            scatter(k, d).wait_send()
        for q in range(orb_n):
            pl.when(jnp.logical_and(z + 1 < orb_n, q <= z))(lambda: line(k, q, True).wait_send())
            pl.when(jnp.logical_and(z >= 1, q >= z))(lambda: line(k, q, False).wait_send())
        for hop in range(1, hops + 1):
            for side in (0, 1):
                on_side(k, hop, side, lambda: ring(k, hop, side).wait_send())
        for j in range(chips):
            pair(k, j).wait_send()
            pair_in(k, j).wait_recv()
        return carry

    lax.fori_loop(0, chunks, finish, 0)


def gather(terms, own, row_n, orb_n):
    vectors, rows, count = terms.shape
    block = rows // orb_n
    chips, chunks, width = row_n // CORES, vectors * SPLIT, count // SPLIT
    dma = pltpu.SemaphoreType.DMA
    return pl.pallas_call(
        functools.partial(gather_kernel, (row_n, orb_n, SPLIT)),
        out_shape=jax.ShapeDtypeStruct((row_n * rows, vectors * count), jnp.bfloat16),
        in_specs=[pl.BlockSpec(memory_space=pl.ANY), pl.BlockSpec(memory_space=pltpu.VMEM)],
        out_specs=pl.BlockSpec(memory_space=pl.ANY),
        scratch_shapes=[
            pltpu.VMEM((chunks, block, width), jnp.bfloat16),
            pltpu.VMEM((chunks, orb_n - 1, block, width), jnp.bfloat16),
            dma((chunks, orb_n - 1)),
            dma((chunks, orb_n - 1)),
            dma((chunks, orb_n)),
            dma((chunks, orb_n)),
            dma((chunks, orb_n)),
            dma((chunks, 2, chips // 2)),
            dma((chunks, chips)),
            dma((chunks, chips)),
            dma((chunks, chips)),
            dma((chunks,)),
        ],
        compiler_params=pltpu.CompilerParams(
            collective_id=0, has_side_effects=True, vmem_limit_bytes=50 * 1024 * 1024
        ),
    )(terms, own)


def on_device(chol_vectors, orbitals):
    row_n, orb_n = lax.axis_size("row"), lax.axis_size("orb")
    block = chol_vectors.shape[1] // orb_n

    def half_transform(vectors):
        return jnp.einsum("prm,mi->pri", vectors, orbitals, preferred_element_type=jnp.float32)

    terms = half_transform(chol_vectors).astype(jnp.bfloat16)
    z = lax.axis_index("orb")
    own = half_transform(lax.dynamic_slice_in_dim(chol_vectors, z * block, block, axis=1))
    whole = gather(terms, own, row_n, orb_n)
    place = (lax.axis_index("row") * orb_n + z) * block
    mine = lax.dynamic_slice_in_dim(whole, place, block, axis=0)
    return lax.dot_general(mine, whole, (((1,), (1,)), ((), ())), preferred_element_type=jnp.float32)


def solution(mesh):
    return jax.shard_map(
        on_device,
        mesh=mesh,
        in_specs=(P(None, "row", "orb"), P("orb", None)),
        out_specs=P(("row", "orb"), None),
        check_vma=False,
    )
```

time: 1010 us -> 473 us (0.47)
  waiting for transfers between devices: 926 us -> 0 us
  Pallas kernels: 0 us -> 410 us
  local copies, waits for them, and re-layouts: 20 us -> 0.13 us
  between operations: 13.1 us -> 0.01 us
  matrix products: 51.1 us -> 63.2 us
    reduce_scatter x2 -> x0, waiting for transfers between devices: 835 us -> none  [the longest x1 552 us: on_device(): lax.psum_scatter(partial_value, 'orb', scatter_dimension=0, tiled=True)]
    pallas_call x0 -> x1, Pallas kernels: none -> 410 us  [gather(): pl.pallas_call(functools.partial(gather_kernel, (row_n, orb_n, SPLIT)), o...]
    all_gather x1 -> x0, waiting for transfers between devices: 90.5 us -> none  [on_device(): lax.all_gather(blocks_local, 'row', axis=1, tiled=True)]
    reshape x2 -> x0, local copies, waits for them, and re-layouts: 20 us -> none  [the longest x1 17.5 us: on_device(): term.reshape(own_orbitals * lax.axis_size('orb'), vectors * row_count)]
    dot_general x2 -> x3, matrix products: 51.1 us -> 63.2 us  [the longest x1 33.8 us: on_device(): lax.dot_general(mine, whole, (((1,), (1,)), ((), ())), preferred_element_...]
  transfers between devices with their start and end apart: 3 -> 0, of which waited for: 3 -> 0; matrix products, arithmetic and copies ran while one was open for 0% -> 0% of each run, Pallas kernels for 0% -> 0%
where the time goes in v1:
time: 473 us
  Pallas kernels  410 us (87%)
  matrix products  63.2 us (13%)
    pallas_call x1, Pallas kernels, gather(): pl.pallas_call(functools.partial(gather_kernel, (row_n, orb_n, SPLIT)), o...  410 us
    dot_general x1, matrix products, on_device(): lax.dot_general(mine, whole, (((1,), (1,)), ((), ())), preferred_element_...  33.8 us
    dot_general x2, matrix products, half_transform(): jnp.einsum('prm,mi->pri', vectors, orbitals, preferred_element_type=jnp.f...  29.4 us

profile of v1, /device:TPU:0, one launch (start us, length us, event | category | flops | bytes accessed | tf_op | source)
XLA Modules:
  0.0 473.1 jit_solution(17204076214040154154)
XLA Ops:
  0.0 0.0 copy-start
  0.0 0.0 copy-start.1
  0.0 10.1 %fusion.own = f32[4,256,1024]{2,1,0:T(8,128)} fusion(bf16[2048,1024]{1,0:T(8,128)(2,1)} %param.3, bf16[4,1024,2048]{2,1,0:T(8,128)(2,1)} %param.2, s32[]{:T(128)S(6)} %select_n.6), kind=kOutput, calls=%fused_computation.1 | convolution fusion | flops 4294967296 | bytes 12582916 | tf_op jit(solution)/shard_map/prm,mi->pri/dot_general | solution.py:223
  10.1 0.0 copy-done
  10.1 0.1 copy-done.1
  10.2 19.3 %convolution_convert_fusion.terms = bf16[4,1024,1024]{2,1,0:T(8,128)(2,1)} fusion(bf16[4,1024,2048]{2,1,0:T(8,128)(2,1)S(1)} %copy-done, bf16[2048,1024]{1,0:T(8,128)(2,1)S(1)} %copy-done.1), kind=kOutput, calls=%fused_computation | convolution fusion | flops 17184063488 | bytes 29360128 | tf_op jit(solution)/shard_map/prm,mi->pri/dot_general | solution.py:223
  29.5 409.7 %shard_map.28 = bf16[8192,4096]{1,0:T(8,128)(2,1)} custom-call(bf16[4,1024,1024]{2,1,0:T(8,128)(2,1)} %convolution_convert_fusion.terms, f32[4,256,1024]{2,1,0:T(8,128)} %fusion.own), custom_call_target="tpu_custom_call" | custom-call | tf_op jit(solution)/shard_map/pallas_call | solution.py:193
  439.2 33.8 %fusion.4 = f32[256,8192]{1,0:T(8,128)} fusion(bf16[8192,4096]{1,0:T(8,128)(2,1)} %shard_map.28, s32[]{:T(128)S(6)} %select_n.7), kind=kOutput, calls=%fused_computation.5 | convolution fusion | flops 17179869184 | bytes 77594624 | tf_op jit(solution)/shard_map/dot_general | solution.py:231
Async XLA Ops:
  0.0 10.1 %copy-start = (bf16[4,1024,2048]{2,1,0:T(8,128)(2,1)S(1)}, bf16[4,1024,2048]{2,1,0:T(8,128)(2,1)}, u32[]{:S(2)}) copy-start(bf16[4,1024,2048]{2,1,0:T(8,128)(2,1)} %param.2) | copy-start | bytes 50331652
  0.0 10.2 %copy-start.1 = (bf16[2048,1024]{1,0:T(8,128)(2,1)S(1)}, bf16[2048,1024]{1,0:T(8,128)(2,1)}, u32[]{:S(2)}) copy-start(bf16[2048,1024]{1,0:T(8,128)(2,1)} %param.3) | copy-start | bytes 12582916

commit v2 on v1

--- a/solution.py
+++ b/solution.py
@@ -9,7 +9,7 @@
 
 MESH = pl.DeviceIdType.MESH
 CORES = 2
-SPLIT = 2
+SPLIT = 4
 
 
 def snake(place, count):
@@ -18,12 +18,14 @@
 
 
 def gather_kernel(
-    sizes, terms, own, out, stage, landed,
-    sum_s, sum_r, up_s, down_s, line_r, ring_s, ring_r, pair_s, pair_r, local_s,
+    sizes, vectors_ref, orbitals, out, held, terms, own, stage, landed, passing, load_s,
+    sum_s, sum_r, pass_r, up_s, down_s, line_r, ring_s, ring_r, pair_s, pair_r, local_s,
 ):
     row_n, orb_n, split = sizes
     chips = row_n // CORES
-    vectors, block, count = own.shape
+    vectors, rows_n, depth = vectors_ref.shape
+    count = orbitals.shape[1]
+    block = rows_n // orb_n
     width = count // split
     chunks = vectors * split
     row, z = lax.axis_index("row"), lax.axis_index("orb")
@@ -58,10 +60,45 @@
             src_ref=src, dst_ref=dst, send_sem=send, recv_sem=recv, device_id=device, device_id_type=MESH
         )
 
-    def scatter(k, d):
-        to = (z + d) % orb_n
-        src = terms.at[k // split, pl.ds(pl.multiple_of(to * block, block), block), columns(k % split)]
-        return remote(src, landed.at[k, d - 1], sum_s.at[k, d - 1], sum_r.at[k, d - 1], (row, to))
+    def far(a, b):
+        d = jnp.maximum(a - b, b - a)
+        return jnp.logical_and(d >= 3, d % 2 == 1)
+
+    def relays(o):
+        d = jnp.maximum(z - o, o - z)
+        outer = jnp.logical_or(
+            jnp.logical_and(z > o, z + 1 < orb_n), jnp.logical_and(z < o, z >= 1)
+        )
+        return jnp.logical_and(jnp.logical_and(d >= 2, d % 2 == 0), outer)
+
+    def to_owner(k, o):
+        return remote(terms.at[k, o], landed.at[k, z], sum_s.at[k, o], sum_r.at[k, z], (row, o))
+
+    def to_relay(k, o):
+        nearer = jnp.where(z > o, z - 1, z + 1)
+        return remote(terms.at[k, o], passing.at[k, o], sum_s.at[k, o], pass_r.at[k, o], (row, nearer))
+
+    def from_source(k, q):
+        return remote(terms.at[k, q], landed.at[k, q], sum_s.at[k, q], sum_r.at[k, q], (row, q))
+
+    def from_outer(k, o):
+        return remote(terms.at[k, o], passing.at[k, o], sum_s.at[k, o], pass_r.at[k, o], (row, o))
+
+    def relay(k):
+        for o in range(orb_n):
+            @pl.when(relays(o))
+            def _():
+                from_outer(k, o).wait_recv()
+                rows = 32
+
+                def one(i, carry):
+                    at_rows = pl.ds(pl.multiple_of(i * rows, rows), rows)
+                    value = own[k % 2, o, at_rows, :] + passing[k, o, at_rows, :].astype(jnp.float32)
+                    terms[k, o, at_rows, :] = value.astype(jnp.bfloat16)
+                    return carry
+
+                lax.fori_loop(0, block // rows, one, 0)
+                to_owner(k, o).start()
 
     def line(k, q, up, first=False):
         src = stage.at[k] if first else part(k, row, q)
@@ -104,43 +141,75 @@
         else:
             pl.when(k % 2 == side)(act)
 
+    def takes(q):
+        return jnp.logical_and(z != q, jnp.logical_not(far(q, z)))
+
     def total(k):
         rows = 32
+
+        def add(q):
+            def one(i, carry):
+                at_rows = pl.ds(pl.multiple_of(i * rows, rows), rows)
+                own[k % 2, z, at_rows, :] += landed[k, q, at_rows, :].astype(jnp.float32)
+                return carry
+
+            lax.fori_loop(0, block // rows, one, 0)
+
+        for q in range(orb_n):
+            @pl.when(takes(q))
+            def _():
+                from_source(k, q).wait_recv()
+                add(q)
+
         def one(i, carry):
             at_rows = pl.ds(pl.multiple_of(i * rows, rows), rows)
-            value = own[k // split, at_rows, columns(k % split)]
-            for d in range(orb_n - 1):
-                value = value + landed[k, d, at_rows, :].astype(jnp.float32)
-            stage[k, at_rows, :] = value.astype(jnp.bfloat16)
+            stage[k, at_rows, :] = own[k % 2, z, at_rows, :].astype(jnp.bfloat16)
             return carry
+
         lax.fori_loop(0, block // rows, one, 0)
 
-    for d in range(1, orb_n):
-        scatter(0, d).start()
+    def load(p):
+        return pltpu.make_async_copy(vectors_ref.at[p], held.at[p % 2], load_s.at[p % 2])
+
+    def begin(k):
+        p = k // split
+
+        @pl.when(k % split == 0)
+        def _():
+            load(p).wait()
+            pl.when(p + 1 < vectors)(lambda: load(p + 1).start())
+
+        def one(q, carry):
+            value = jnp.dot(
+                held[p % 2, pl.ds(pl.multiple_of(q * block, block), block), :],
+                orbitals[:, columns(k % split)],
+                preferred_element_type=jnp.float32,
+            )
+            terms[k, q] = value.astype(jnp.bfloat16)
+            own[k % 2, q] = value
+
+            return carry
+
+        lax.fori_loop(0, orb_n, one, 0)
+        for o in range(orb_n):
+            pl.when(far(o, z))(lambda: to_relay(k, o).start())
+        for o in range(orb_n):
+            near = jnp.logical_and(takes(o), jnp.logical_not(relays(o)))
+            pl.when(near)(lambda: to_owner(k, o).start())
+
+    load(0).start()
+    begin(0)
+    relay(0)
 
     def step(t, carry):
-        before = t - 1
-
-        @pl.when(t < chunks - 1)
-        def _():
-            for d in range(1, orb_n):
-                scatter(t + 1, d).start()
-
         @pl.when(t < chunks)
         def _():
-            for d in range(1, orb_n):
-                scatter(t, d).wait_recv()
             total(t)
             keep(t).start()
             pl.when(z + 1 < orb_n)(lambda: line(t, z, True, True).start())
             pl.when(z >= 1)(lambda: line(t, z, False, True).start())
 
-        @pl.when(t >= 1)
-        def _():
-            for hop in range(1, hops):
-                for side in (0, 1):
-                    arrived(before, hop, side)
-                    on_side(before, hop + 1, side, lambda: ring(before, hop + 1, side).start())
+        pl.when(t < chunks - 1)(lambda: begin(t + 1))
 
         @pl.when(t < chunks)
         def _():
@@ -159,18 +228,28 @@
                 on_side(t, 1, side, lambda: ring(t, 1, side).start())
             pair(t, 0).start()
 
-        @pl.when(t >= 1)
+        pl.when(t < chunks - 1)(lambda: relay(t + 1))
+
+        @pl.when(jnp.logical_and(t >= 1, t <= chunks))
+        def _():
+            for hop in range(1, hops):
+                for side in (0, 1):
+                    arrived(t - 1, hop, side)
+                    on_side(t - 1, hop + 1, side, lambda: ring(t - 1, hop + 1, side).start())
+
+        @pl.when(t >= 2)
         def _():
             for side in (0, 1):
-                on_side(before, hops, side, lambda: arrived(before, hops, side))
+                on_side(t - 2, hops, side, lambda: arrived(t - 2, hops, side))
 
         return carry
 
-    lax.fori_loop(0, chunks + 1, step, 0)
+    lax.fori_loop(0, chunks + 2, step, 0)
 
     def finish(k, carry):
-        for d in range(1, orb_n):
-            scatter(k, d).wait_send()
+        for o in range(orb_n):
+            pl.when(far(o, z))(lambda: to_relay(k, o).wait_send())
+            pl.when(takes(o))(lambda: to_owner(k, o).wait_send())
         for q in range(orb_n):
             pl.when(jnp.logical_and(z + 1 < orb_n, q <= z))(lambda: line(k, q, True).wait_send())
             pl.when(jnp.logical_and(z >= 1, q >= z))(lambda: line(k, q, False).wait_send())
@@ -185,8 +264,9 @@
     lax.fori_loop(0, chunks, finish, 0)
 
 
-def gather(terms, own, row_n, orb_n):
-    vectors, rows, count = terms.shape
+def gather(chol_vectors, orbitals, row_n, orb_n):
+    vectors, rows, depth = chol_vectors.shape
+    count = orbitals.shape[1]
     block = rows // orb_n
     chips, chunks, width = row_n // CORES, vectors * SPLIT, count // SPLIT
     dma = pltpu.SemaphoreType.DMA
@@ -196,10 +276,16 @@
         in_specs=[pl.BlockSpec(memory_space=pl.ANY), pl.BlockSpec(memory_space=pltpu.VMEM)],
         out_specs=pl.BlockSpec(memory_space=pl.ANY),
         scratch_shapes=[
+            pltpu.VMEM((2, rows, depth), jnp.bfloat16),
+            pltpu.VMEM((chunks, orb_n, block, width), jnp.bfloat16),
+            pltpu.VMEM((2, orb_n, block, width), jnp.float32),
             pltpu.VMEM((chunks, block, width), jnp.bfloat16),
-            pltpu.VMEM((chunks, orb_n - 1, block, width), jnp.bfloat16),
-            dma((chunks, orb_n - 1)),
-            dma((chunks, orb_n - 1)),
+            pltpu.VMEM((chunks, orb_n, block, width), jnp.bfloat16),
+            pltpu.VMEM((chunks, orb_n, block, width), jnp.bfloat16),
+            dma((2,)),
+            dma((chunks, orb_n)),
+            dma((chunks, orb_n)),
+            dma((chunks, orb_n)),
             dma((chunks, orb_n)),
             dma((chunks, orb_n)),
             dma((chunks, orb_n)),
@@ -210,22 +296,17 @@
             dma((chunks,)),
         ],
         compiler_params=pltpu.CompilerParams(
-            collective_id=0, has_side_effects=True, vmem_limit_bytes=50 * 1024 * 1024
+            collective_id=0, has_side_effects=True, vmem_limit_bytes=56 * 1024 * 1024
         ),
-    )(terms, own)
+    )(chol_vectors, orbitals)
 
 
 def on_device(chol_vectors, orbitals):
     row_n, orb_n = lax.axis_size("row"), lax.axis_size("orb")
     block = chol_vectors.shape[1] // orb_n
 
-    def half_transform(vectors):
-        return jnp.einsum("prm,mi->pri", vectors, orbitals, preferred_element_type=jnp.float32)
-
-    terms = half_transform(chol_vectors).astype(jnp.bfloat16)
     z = lax.axis_index("orb")
-    own = half_transform(lax.dynamic_slice_in_dim(chol_vectors, z * block, block, axis=1))
-    whole = gather(terms, own, row_n, orb_n)
+    whole = gather(chol_vectors, orbitals, row_n, orb_n)
     place = (lax.axis_index("row") * orb_n + z) * block
     mine = lax.dynamic_slice_in_dim(whole, place, block, axis=0)
     return lax.dot_general(mine, whole, (((1,), (1,)), ((), ())), preferred_element_type=jnp.float32)

time: 473 us -> 372 us (0.79)
  Pallas kernels: 410 us -> 338 us
  matrix products: 63.2 us -> 33.9 us
    pallas_call x1, Pallas kernels: 410 us -> 338 us  [gather(): pl.pallas_call(functools.partial(gather_kernel, (row_n, orb_n, SPLIT)), o...]
    dot_general x2 -> x0, matrix products: 29.4 us -> none  [half_transform(): jnp.einsum('prm,mi->pri', vectors, orbitals, preferred_element_type=jnp.f...]
where the time goes in v2:
time: 372 us; the launch traced here: 371 us
  Pallas kernels  338 us (91%)
  matrix products  33.9 us (9%)
    pallas_call x1, Pallas kernels, gather(): pl.pallas_call(functools.partial(gather_kernel, (row_n, orb_n, SPLIT)), o...  338 us
    dot_general x1, matrix products, on_device(): lax.dot_general(mine, whole, (((1,), (1,)), ((), ())), preferred_element_...  33.9 us

profile of v2, /device:TPU:0, one launch (start us, length us, event | category | flops | bytes accessed | tf_op | source)
XLA Modules:
  0.0 371.4 jit_solution(1375726477032644532)
XLA Ops:
  0.0 337.5 %shard_map.28 = bf16[8192,4096]{1,0:T(8,128)(2,1)} custom-call(bf16[4,1024,2048]{2,1,0:T(8,128)(2,1)} %vectors_ref.1, bf16[2048,1024]{1,0:T(8,128)(2,1)} %orbitals.1), custom_call_target="tpu_custom_call" | custom-call | tf_op jit(solution)/shard_map/pallas_call | solution.py:273
  337.5 33.9 %fusion = f32[256,8192]{1,0:T(8,128)} fusion(bf16[8192,4096]{1,0:T(8,128)(2,1)} %shard_map.28, s32[]{:T(128)S(6)} %select_n.3), kind=kOutput, calls=%fused_computation | convolution fusion | flops 17179869184 | bytes 77594624 | tf_op jit(solution)/shard_map/dot_general | solution.py:312
